TPU v7x, 32 devices: a whole 2x2x4 slice. The times are simulated.
32 devices in a mesh: sec: 4 (over x, core), tile: 8 (over z, y).
Axes of the slice: x: 2, y: 2, z: 4, core: 2. Of those that a mesh axis runs over, the one named last changes fastest.
Arguments:
- intersection_faces: bfloat16 [256, 1, 128, 128], P(('sec', 'tile')), may hold values from -6 to 6
- destination: int32 [256, 1], P(('sec', 'tile')), may hold values from 0 to 7; in each aligned block of 8 rows (0 to 7, 8 to 15, ...) at most 2 rows name the same one
- partner: int32 [256], P(('sec', 'tile')), may hold values from 0 to 7
- face_peaks: int32 [256, 2, 8], P(('sec', 'tile')), may hold values from 0 to 127
- coarse: bfloat16 [64, 256, 256], P(('sec', 'tile')), may hold values from -6 to 6
- coarse_peaks: int32 [256, 2, 8], P(('sec', 'tile')), may hold values from 0 to 255
- upper_faces: bfloat16 [64, 1, 128, 128], P(('sec', 'tile')), may hold values from -6 to 6
- lower_faces: bfloat16 [64, 1, 128, 128], P(('sec', 'tile')), may hold values from -6 to 6
- section_peaks: int32 [64, 2, 8], P(('sec', 'tile')), may hold values from 0 to 127
Outputs:
- fine_scores: float32 [256, 1, 8], P(('sec', 'tile'))
- coarse_scores: float32 [256, 8], P(('sec', 'tile'))
- section_scores: float32 [64, 1, 8], P(('sec', 'tile'))
Inputs may be any that keep to these rules, and one draw needn't show every extreme that they name: `destination`: in each aligned block of 8 rows (the faces of one device) no value appears more than 2 times.
All inputs are finite; a program needn't handle non-finite values.
Results may differ from a plain program's by a relative error of at most 0.012.
The roundings to bfloat16 on the way count: a program that leaves them out, or rounds other values in their place, can miss the bound.
Values may be sent and summed in bfloat16 or wider, within the bound.
A program may use at most 64 MiB of HBM per device.

v0:
```python
import jax
import jax.numpy as jnp
from jax import lax
from jax.sharding import PartitionSpec as P

TWO_PI = 6.283185307179586


def from_behind(value, axis, steps):
    count = lax.axis_size(axis)
    first, last = (max(0, -steps), min(count, count - steps))
    return lax.ppermute(value, axis, [(source, source + steps) for source in range(first, last)])


def window_weights(extent):
    positions = jnp.arange(extent, dtype=jnp.float32)
    return 0.5 - 0.5 * jnp.cos((positions + 0.5) * (TWO_PI / extent))


def dft_tables(extent):
    indices = jnp.arange(extent, dtype=jnp.int32)
    angles = (indices[:, None] * indices[None, :] % extent).astype(jnp.float32) * (TWO_PI / extent)
    return (jnp.cos(angles).astype(jnp.bfloat16), jnp.sin(angles).astype(jnp.bfloat16))


def spectrum(images):
    extent = images.shape[-1]
    weights = window_weights(extent)
    shaped = (images.astype(jnp.float32) * weights[:, None] * weights[None, :]).astype(jnp.bfloat16)
    cosine, sine_table = dft_tables(extent)
    segment_tables = jnp.stack([cosine, sine_table])
    segment_one = jnp.einsum(
        "jkx,...xy->...jky", segment_tables, shaped, preferred_element_type=jnp.float32
    ).astype(jnp.bfloat16)
    second_tables = jnp.stack(
        [
            jnp.concatenate([cosine, sine_table], axis=1),
            jnp.concatenate([-sine_table, cosine], axis=1),
        ]
    )
    segment_two = jnp.einsum(
        "...jky,jyl->...kl", segment_one, second_tables, preferred_element_type=jnp.float32
    )
    return (segment_two[..., :extent], -segment_two[..., extent:])


def correlate(own_spec, other_spec, peak_marks):
    own_real, own_imag = own_spec
    other_real, other_imag = other_spec
    cross_real = own_real * other_real + own_imag * other_imag
    cross_imag = own_imag * other_real - own_real * other_imag
    magnitude = jnp.sqrt(cross_real * cross_real + cross_imag * cross_imag)
    floor_value = 0.05 * jnp.mean(magnitude, axis=(-2, -1), keepdims=True) + 1e-06
    divisor = jnp.maximum(magnitude, floor_value)
    unit_real = cross_real / divisor
    unit_imag = cross_imag / divisor
    extent = own_real.shape[-1]
    indices = jnp.arange(extent, dtype=jnp.int32)
    row_angles = (peak_marks[..., 0, :, None] * indices % extent).astype(jnp.float32) * (
        TWO_PI / extent
    )
    col_angles = (peak_marks[..., 1, :, None] * indices % extent).astype(jnp.float32) * (
        TWO_PI / extent
    )
    row_cos = jnp.cos(row_angles)
    row_sin = jnp.sin(row_angles)
    high = lax.Precision.HIGHEST
    first_real = jnp.einsum("...pk,...kl->...pl", row_cos, unit_real, precision=high) - jnp.einsum(
        "...pk,...kl->...pl", row_sin, unit_imag, precision=high
    )
    first_imag = jnp.einsum("...pk,...kl->...pl", row_cos, unit_imag, precision=high) + jnp.einsum(
        "...pk,...kl->...pl", row_sin, unit_real, precision=high
    )
    return (
        jnp.sum(first_real * jnp.cos(col_angles) - first_imag * jnp.sin(col_angles), axis=-1)
        / extent
    )


def body(
    intersection_faces,
    destination,
    partner,
    face_peaks,
    coarse,
    coarse_peaks,
    upper_faces,
    lower_faces,
    section_peaks,
):
    face_dev = intersection_faces.shape[0]
    tile_dev = coarse.shape[0]
    per_tile = face_dev // tile_dev
    windows = intersection_faces.shape[1]
    peak_count = face_peaks.shape[2]
    coarse_side = coarse.shape[-1]
    tile_count = lax.axis_size("tile")
    capacity = max(2, (face_dev + tile_count - 1) // tile_count)
    slot_count = tile_count * capacity
    target = destination[:, 0]
    face_order = jnp.arange(face_dev, dtype=jnp.int32)
    earlier = (target[None, :] == target[:, None]) & (face_order[None, :] < face_order[:, None])
    position = jnp.sum(earlier.astype(jnp.int32), axis=1)
    slot_of = target * capacity + position
    slot_match = slot_of[None, :] == jnp.arange(slot_count, dtype=jnp.int32)[:, None]
    filled = jnp.any(slot_match, axis=1)
    source = jnp.sum(jnp.where(slot_match, face_order[None, :], 0), axis=1)
    requests = jnp.where(filled, partner[source] + 1, 0).reshape(tile_count, capacity)
    own_real, own_imag = spectrum(intersection_faces)
    parcel = jnp.where(
        filled[:, None, None, None],
        intersection_faces[source],
        jnp.zeros_like(intersection_faces[source]),
    )
    parcel = parcel.reshape((tile_count, capacity) + intersection_faces.shape[1:])
    peak_marks = face_peaks[source].reshape((tile_count, capacity) + face_peaks.shape[1:])
    got_faces, got_marks, wanted_ids = (
        lax.all_to_all(parcel, "tile", split_axis=0, concat_axis=0, tiled=True),
        lax.all_to_all(peak_marks, "tile", split_axis=0, concat_axis=0, tiled=True),
        lax.all_to_all(requests, "tile", split_axis=0, concat_axis=0, tiled=True),
    )

    def one_slot(packed):
        face_in, mark_in, wanted = packed
        chosen_slot = jnp.maximum(wanted - 1, 0)
        own_part = (own_real[chosen_slot], own_imag[chosen_slot])
        marks_all = mark_in[None]
        scores = correlate(spectrum(face_in), own_part, marks_all)
        return jnp.where(wanted > 0, scores, jnp.zeros_like(scores))

    slot_scores = lax.map(
        one_slot,
        (
            got_faces.reshape((slot_count,) + intersection_faces.shape[1:]),
            got_marks.reshape((slot_count,) + face_peaks.shape[1:]),
            wanted_ids.reshape(slot_count),
        ),
    )
    returned = lax.all_to_all(
        slot_scores.reshape(tile_count, capacity, windows, peak_count),
        "tile",
        split_axis=0,
        concat_axis=0,
        tiled=True,
    )
    fine_scores = returned.reshape(slot_count, windows, peak_count)[slot_of]
    coarse_real, coarse_imag = spectrum(coarse)
    wanted_tile = target * tile_dev + partner // per_tile
    empty_tiles = jnp.zeros((face_dev, coarse_side, coarse_side), jnp.bfloat16)
    shard_rows = lax.all_gather(coarse, "tile", axis=0, tiled=True)
    row_count = shard_rows.shape[0]
    inside = (wanted_tile >= 0) & (wanted_tile < row_count)
    selected = shard_rows[jnp.clip(wanted_tile, 0, row_count - 1)]
    partner_tiles = jnp.where(inside[:, None, None], selected, empty_tiles)

    def coarse_one(packed):
        tile_slot, other_tile, mark_in = packed
        return correlate(
            (coarse_real[tile_slot], coarse_imag[tile_slot]), spectrum(other_tile), mark_in
        )

    coarse_scores = lax.map(coarse_one, (face_order // per_tile, partner_tiles, coarse_peaks))
    lower_in = from_behind(lower_faces, "sec", 1)
    section_marks = section_peaks[:, None]
    section_scores = correlate(spectrum(upper_faces), spectrum(lower_in), section_marks)
    return (fine_scores, coarse_scores, section_scores)


def solution(mesh):
    return jax.shard_map(
        body,
        mesh=mesh,
        in_specs=(
            P(("sec", "tile"), None, None, None),
            P(("sec", "tile"), None),
            P(("sec", "tile")),
            P(("sec", "tile"), None, None),
            P(("sec", "tile"), None, None),
            P(("sec", "tile"), None, None),
            P(("sec", "tile"), None, None, None),
            P(("sec", "tile"), None, None, None),
            P(("sec", "tile"), None, None),
        ),
        out_specs=(
            P(("sec", "tile"), None, None),
            P(("sec", "tile"), None),
            P(("sec", "tile"), None, None),
        ),
        check_vma=False,
    )
```

profile of v0, /device:TPU:0, one launch (start us, length us, event | category | flops | bytes accessed | tf_op | source)
XLA Modules:
  0.0 286.7 jit_solution(2886775491009147244)
XLA Ops:
  9.7 1.3 gather_fusion
  11.7 7.3 %all-to-all-start = ((s32[8,1,2]{2,1,0:T(1,128)}), s32[8,1,2]{2,1,0:T(1,128)}, u32[]{:S(2)}, u32[]{:S(2)}) async-start(s32[8,1,2]{2,1,0:T(1,128)} %bitcast.34), calls=%async_computation | async-start | bytes 8192 | tf_op jit(solution)/shard_map/all_to_all | solution.py:120
  19.0 2.1 collective-permute-start
  27.7 1.4 fusion.275
  34.7 1.6 broadcast_select_fusion.2
  38.1 5.8 %all-to-all-start.1 = ((s32[8,2,2,8]{3,2,1,0:T(2,128)}), s32[8,2,2,8]{3,2,1,0:T(2,128)S(1)}, u32[]{:S(2)}, u32[]{:S(2)}) async-start(s32[8,2,2,8]{3,2,1,0:T(2,128)} %bitcast.35), calls=%async_computation.1 | async-start | bytes 32768 | tf_op jit(solution)/shard_map/all_to_all | solution.py:119
  44.5 1.3 reduce.15
  45.9 1.4 convolution_bitcast_fusion.4
  47.4 3.3 %all-to-all-done.1 = s32[8,2,2,8]{3,2,1,0:T(2,128)S(1)} async-done(((s32[8,2,2,8]{3,2,1,0:T(2,128)}), s32[8,2,2,8]{3,2,1,0:T(2,128)S(1)}, u32[]{:S(2)}, u32[]{:S(2)}) %all-to-all-start.1) | async-done | bytes 1056 | tf_op jit(solution)/shard_map/all_to_all | solution.py:119
  50.7 3.5 %all-to-all-start.2 = ((bf16[8,2,1,128,128]{3,4,1,2,0:T(8,128)(2,1)}), bf16[8,2,1,128,128]{3,4,1,2,0:T(8,128)(2,1)S(1)}, u32[]{:S(2)}, u32[]{:S(2)}) async-start(bf16[8,2,1,128,128]{3,4,1,2,0:T(8,128)(2,1)} %broadcast_select_fusion.2), calls=%async_computation.2 | async-start | bytes 1048576 | tf_op jit(solution)/shard_map/all_to_all | solution.py:118
  55.7 17.7 %all-to-all-done.2 = bf16[8,2,1,128,128]{3,4,1,2,0:T(8,128)(2,1)S(1)} async-done(((bf16[8,2,1,128,128]{3,4,1,2,0:T(8,128)(2,1)}), bf16[8,2,1,128,128]{3,4,1,2,0:T(8,128)(2,1)S(1)}, u32[]{:S(2)}, u32[]{:S(2)}) %all-to-all-start.2) | async-done | bytes 524320 | tf_op jit(solution)/shard_map/all_to_all | solution.py:118
  73.4 112.0 %while.24 = (s32[]{:T(128)}, f32[16,1,8]{2,1,0:T(1,128)}, s32[16]{0:T(128)S(1)}, s32[16,2,8]{2,1,0:T(2,128)S(1)}, bf16[16,1,128,128]{2,3,1,0:T(8,128)(2,1)S(1)},...) while((s32[]{:T(128)}, f32[16,1,8]{2,1,0:T(1,128)}, ...), condition=%wide.region_6.7_spmd, body=%wide.region_3.6_spmd.sunk | while | flops 33161740 | bytes 1723514 | solution.py:131
  76.9 1.5 fusion.332
  83.9 1.5 fusion.332
  90.9 1.5 fusion.332
  97.8 1.5 fusion.332
  104.8 1.5 fusion.332
  111.8 1.5 fusion.332
  118.8 1.5 fusion.332
  125.8 1.5 fusion.332
  132.8 1.5 fusion.332
  139.8 1.5 fusion.332
  146.7 1.5 fusion.332
  153.8 1.5 fusion.332
  160.8 1.5 fusion.332
  167.8 1.5 fusion.332
  174.8 1.5 fusion.332
  181.8 1.5 fusion.332
  185.4 3.6 %all-to-all-start.3 = ((f32[8,2,1,8]{3,1,2,0:T(2,128)}), f32[8,2,1,8]{3,1,2,0:T(2,128)S(1)}, u32[]{:S(2)}, u32[]{:S(2)}) async-start(f32[8,2,1,8]{3,1,2,0:T(2,128)} %bitcast.56), calls=%async_computation.3 | async-start | bytes 16384 | tf_op jit(solution)/shard_map/all_to_all | solution.py:139
  189.6 5.7 %all-to-all-done.3 = f32[8,2,1,8]{3,1,2,0:T(2,128)S(1)} async-done(((f32[8,2,1,8]{3,1,2,0:T(2,128)}), f32[8,2,1,8]{3,1,2,0:T(2,128)S(1)}, u32[]{:S(2)}, u32[]{:S(2)}) %all-to-all-start.3) | async-done | bytes 544 | tf_op jit(solution)/shard_map/all_to_all | solution.py:139
  196.6 2.3 gather_fusion.4
  199.1 80.1 %while.25 = (s32[]{:T(128)}, f32[8,8]{1,0:T(8,128)S(1)}, s32[8,2,8]{2,1,0:T(2,128)}, s32[8]{0:T(128)S(1)}, f32[2,256,256]{2,1,0:T(8,128)S(1)}, /*index=5*/bf16[8...) while((s32[]{:T(128)}, f32[8,8]{1,0:T(8,128)S(1)}, ...), condition=%wide.region_10.11_spmd, body=%wide.region_7.10_spmd.sunk | while | flops 232903680 | bytes 6737723 | solution.py:162
  (468 shorter events, 136.5 us)
Async XLA Ops:
  7.2 29.6 %copy-start = (s32[8,2,8]{2,1,0:T(2,128)S(1)}, s32[8,2,8]{2,1,0:T(2,128)}, u32[]{:S(2)}) copy-start(s32[8,2,8]{2,1,0:T(2,128)} %param.16) | copy-start | bytes 1540
  7.2 23.1 %copy-start.4 = (bf16[2,256,256]{2,1,0:T(8,128)(2,1)S(1)}, bf16[2,256,256]{2,1,0:T(8,128)(2,1)}, u32[]{:S(2)}) copy-start(bf16[2,256,256]{2,1,0:T(8,128)(2,1)} %param.17) | copy-start | bytes 786436
  7.2 189.4 %all-gather.2.cloned.1.call-start = ((), (), s32[]{:S(2)}) async-start(), calls=%async_computation.4 | async-start | bytes 2359296 | tf_op jit(solution)/shard_map/all_gather | solution.py:150
  9.7 23.2 %copy-start.7 = (s32[1024]{0:T(1024)}, s32[1024]{0:T(1024)S(1)}, u32[]{:S(2)}) copy-start(s32[1024]{0:T(1024)S(1)} %pad_clamp_fusion.2) | copy-start | bytes 12292
  11.7 26.4 %all-to-all-start = ((s32[8,1,2]{2,1,0:T(1,128)}), s32[8,1,2]{2,1,0:T(1,128)}, u32[]{:S(2)}, u32[]{:S(2)}) async-start(s32[8,1,2]{2,1,0:T(1,128)} %bitcast.34), calls=%async_computation | async-start | bytes 8192 | tf_op jit(solution)/shard_map/all_to_all | solution.py:120
  19.0 26.9 %collective-permute-start = (bf16[2,1,128,128]{3,2,1,0:T(8,128)(2,1)}, bf16[2,1,128,128]{3,2,1,0:T(8,128)(2,1)}, u32[]{:S(2)}, u32[]{:S(2)}) collective-permute-start(bf16[2,1,128,128]{3,2,1,0:T(8,128)(2,1)} %param.20), channel_id=1, source_target_pairs={{0,8},{8,16},{16,24},{1,9},{9,17},{17,25},{2,10},{10,18},{18,26},{... | collective-permute-start | bytes 196616 | tf_op jit(solution)/shard_map/ppermute | solution.py:12
  24.2 8.7 %copy-start.2 = (bf16[1,128,128]{2,1,0:T(8,128)(2,1)}, bf16[1,128,128]{2,1,0:T(8,128)(2,1)S(1)}, u32[]{:S(2)}) copy-start(bf16[1,128,128]{2,1,0:T(8,128)(2,1)S(1)} %get-tuple-element.303) | copy-start | bytes 98308
  24.2 8.7 %copy-start.3 = (bf16[1,128,128]{2,1,0:T(8,128)(2,1)}, bf16[1,128,128]{2,1,0:T(8,128)(2,1)S(1)}, u32[]{:S(2)}) copy-start(bf16[1,128,128]{2,1,0:T(8,128)(2,1)S(1)} %get-tuple-element.304) | copy-start | bytes 98308
  30.3 1.0 copy-start.5
  31.2 1.0 copy-start.1
  34.7 20.3 %copy-start.6 = (s32[2,1,1,8]{3,2,0,1:T(1,128)S(1)}, s32[2,1,1,8]{3,2,0,1:T(1,128)}, u32[]{:S(2)}) copy-start(s32[2,1,1,8]{3,2,0,1:T(1,128)} %get-tuple-element.299) | copy-start | bytes 196
  38.1 12.6 %all-to-all-start.1 = ((s32[8,2,2,8]{3,2,1,0:T(2,128)}), s32[8,2,2,8]{3,2,1,0:T(2,128)S(1)}, u32[]{:S(2)}, u32[]{:S(2)}) async-start(s32[8,2,2,8]{3,2,1,0:T(2,128)} %bitcast.35), calls=%async_computation.1 | async-start | bytes 32768 | tf_op jit(solution)/shard_map/all_to_all | solution.py:119
  50.7 22.7 %all-to-all-start.2 = ((bf16[8,2,1,128,128]{3,4,1,2,0:T(8,128)(2,1)}), bf16[8,2,1,128,128]{3,4,1,2,0:T(8,128)(2,1)S(1)}, u32[]{:S(2)}, u32[]{:S(2)}) async-start(bf16[8,2,1,128,128]{3,4,1,2,0:T(8,128)(2,1)} %broadcast_select_fusion.2), calls=%async_computation.2 | async-start | bytes 1048576 | tf_op jit(solution)/shard_map/all_to_all | solution.py:118
  185.4 13.5 %copy-start.8 = (pred[8]{0:T(512)(128)(4,1)S(1)}, pred[8]{0:T(512)(128)(4,1)}, u32[]{:S(2)}) copy-start(pred[8]{0:T(512)(128)(4,1)} %get-tuple-element.265) | copy-start | bytes 28
  185.4 9.9 %all-to-all-start.3 = ((f32[8,2,1,8]{3,1,2,0:T(2,128)}), f32[8,2,1,8]{3,1,2,0:T(2,128)S(1)}, u32[]{:S(2)}, u32[]{:S(2)}) async-start(f32[8,2,1,8]{3,1,2,0:T(2,128)} %bitcast.56), calls=%async_computation.3 | async-start | bytes 16384 | tf_op jit(solution)/shard_map/all_to_all | solution.py:139
  196.6 2.5 copy-start.9
  196.6 2.5 copy-start.11
  279.2 0.6 copy-start.10
Sparse Core Ops, SparseCore 0:
  10.1 56.0 all-gather.1
where the time goes:
time: 289 us; the launch traced here: 287 us
  other arithmetic  98.8 us (34%)
  loops' own time  53.6 us (19%)
  matrix products  38.8 us (13%)
  local copies, waits for them, and re-layouts  31.4 us (11%)
  waiting for transfers between devices  27.4 us (9%)
  starting transfers between devices  22.3 us (8%)
  between operations  14.3 us (5%)
    another operation x1, loops' own time, body(): lax.map(one_slot, (got_faces.reshape((slot_count,) + intersection_faces.s...  32.3 us
    reduce_sum x25, other arithmetic, correlate(): jnp.mean(magnitude, axis=(-2, -1), keepdims=True)  30.3 us
    convert_element_type x52, other arithmetic, dft_tables(): jnp.sin(angles).astype(jnp.bfloat16)  29.3 us
    another operation x1, loops' own time, body(): lax.map(coarse_one, (face_order // per_tile, partner_tiles, coarse_peaks))  21.4 us
    all_to_all x1, waiting for transfers between devices, body(): lax.all_to_all(parcel, 'tile', split_axis=0, concat_axis=0, tiled=True)  17.7 us
    dot_general x28, matrix products, spectrum(): jnp.einsum('...jky,jyl->...kl', segment_one, second_tables, preferred_ele...  13.9 us
    neg x26, other arithmetic, spectrum(): -sine_table  13.5 us
    dynamic_slice x16, local copies, waits for them, and re-layouts, body(): lax.map(coarse_one, (face_order // per_tile, partner_tiles, coarse_peaks))  10.2 us
  transfers between devices with their start and end apart: 6, of which 3 were waited for; matrix products, arithmetic and copies ran while one was open for 37% of the time, Pallas kernels for 0%

commit v1 on v0

--- a/solution.py
+++ b/solution.py
@@ -4,6 +4,18 @@
 from jax.sharding import PartitionSpec as P
 
 TWO_PI = 6.283185307179586
+
+
+def _produce_vectors(q_in, array_dim, u):
+    w1 = q_in.shape
+    even = q_in.reshape(*w1[:array_dim], u, w1[array_dim] // u, *w1[array_dim + 1 :])
+    return jnp.moveaxis(even, array_dim, 0)
+
+
+def _deliver_edge(local_block, on_dim):
+    mid_arr = list(local_block.shape[1:])
+    mid_arr[on_dim] *= local_block.shape[0]
+    return jnp.moveaxis(local_block, 0, on_dim).reshape(mid_arr)
 
 
 def from_behind(value, axis, steps):
@@ -114,8 +126,23 @@
     )
     parcel = parcel.reshape((tile_count, capacity) + intersection_faces.shape[1:])
     peak_marks = face_peaks[source].reshape((tile_count, capacity) + face_peaks.shape[1:])
+
+    def _balance_stops_all(array_here, peer_axis, arr_in, mine_x):
+        m_next = lax.axis_size(peer_axis)
+        f_now, local_out = (m_next, lax.axis_index(peer_axis))
+        plain = _produce_vectors(array_here, arr_in, f_now)
+        pages = [plain[local_out]]
+        for b in range(1, f_now):
+            current_arr = plain[local_out ^ b]
+            pages.append(
+                lax.ppermute(current_arr, peer_axis, [(k0, k0 ^ b) for k0 in range(f_now)])
+            )
+        v1 = jnp.stack(pages)
+        plain = v1[local_out ^ jnp.arange(f_now)]
+        return _deliver_edge(plain, mine_x)
+
     got_faces, got_marks, wanted_ids = (
-        lax.all_to_all(parcel, "tile", split_axis=0, concat_axis=0, tiled=True),
+        _balance_stops_all(parcel, "tile", 0, 0),
         lax.all_to_all(peak_marks, "tile", split_axis=0, concat_axis=0, tiled=True),
         lax.all_to_all(requests, "tile", split_axis=0, concat_axis=0, tiled=True),
     )

time: 289 us -> 285 us (0.986)
  other arithmetic: 98.8 us -> 83.1 us
  local copies, waits for them, and re-layouts: 31.4 us -> 43.1 us
  waiting for transfers between devices: 27.4 us -> 20.7 us
  starting transfers between devices: 22.3 us -> 28.8 us
    all_to_all x1 -> x0, waiting for transfers between devices: 17.7 us -> none  [body(): lax.all_to_all(parcel, 'tile', split_axis=0, concat_axis=0, tiled=True)]
    ppermute x0 -> x7, waiting for transfers between devices: none -> 17.2 us  [_balance_stops_all(): lax.ppermute(current_arr, peer_axis, [(k0, k0 ^ b) for k0 in range(f_now)])]
    reduce_sum x25, other arithmetic: 30.3 us -> 16.7 us  [correlate(): jnp.mean(magnitude, axis=(-2, -1), keepdims=True)]
    ppermute x0 -> x7, starting transfers between devices: none -> 10.6 us  [_balance_stops_all(): lax.ppermute(current_arr, peer_axis, [(k0, k0 ^ b) for k0 in range(f_now)])]
    unnamed x24 -> x40, local copies, waits for them, and re-layouts: 0.96 us -> 7.28 us
    all_to_all x1 -> x0, starting transfers between devices: 3.49 us -> none  [body(): lax.all_to_all(parcel, 'tile', split_axis=0, concat_axis=0, tiled=True)]
    all_to_all x1, waiting for transfers between devices: 3.28 us -> 0.01 us  [body(): lax.all_to_all(peak_marks, 'tile', split_axis=0, concat_axis=0, tiled=True)]
    dynamic_slice x32 -> x64, local copies, waits for them, and re-layouts: 9.47 us -> 11.4 us  [body(): lax.map(one_slot, (got_faces.reshape((slot_count,) + intersection_faces.s...]
  transfers between devices with their start and end apart: 6 -> 12, of which waited for: 3 -> 4; matrix products, arithmetic and copies ran while one was open for 37% -> 37% of each run, Pallas kernels for 0% -> 0%
where the time goes in v1:
time: 285 us; the launch traced here: 284 us
  other arithmetic  83.1 us (29%)
  loops' own time  53.9 us (19%)
  local copies, waits for them, and re-layouts  43.1 us (15%)
  matrix products  39.8 us (14%)
  starting transfers between devices  28.8 us (10%)
  waiting for transfers between devices  20.7 us (7%)
  between operations  14.4 us (5%)
    another operation x1, loops' own time, body(): lax.map(one_slot, (got_faces.reshape((slot_count,) + intersection_faces.s...  32.5 us
    convert_element_type x52, other arithmetic, dft_tables(): jnp.sin(angles).astype(jnp.bfloat16)  29.9 us
    another operation x1, loops' own time, body(): lax.map(coarse_one, (face_order // per_tile, partner_tiles, coarse_peaks))  21.4 us
    ppermute x7, waiting for transfers between devices, _balance_stops_all(): lax.ppermute(current_arr, peer_axis, [(k0, k0 ^ b) for k0 in range(f_now)])  17.2 us
    reduce_sum x25, other arithmetic, correlate(): jnp.mean(magnitude, axis=(-2, -1), keepdims=True)  16.7 us
    dot_general x28, matrix products, spectrum(): jnp.einsum('...jky,jyl->...kl', segment_one, second_tables, preferred_ele...  14.9 us
    neg x26, other arithmetic, spectrum(): -sine_table  13.6 us
    dynamic_slice x64, local copies, waits for them, and re-layouts, body(): lax.map(one_slot, (got_faces.reshape((slot_count,) + intersection_faces.s...  11.4 us
  transfers between devices with their start and end apart: 12, of which 4 were waited for; matrix products, arithmetic and copies ran while one was open for 37% of the time, Pallas kernels for 0%

profile of v1, /device:TPU:0, one launch (start us, length us, event | category | flops | bytes accessed | tf_op | source)
XLA Modules:
  0.0 283.8 jit_solution(8778719064940338810)
XLA Ops:
  9.7 1.3 gather_fusion
  11.7 7.3 %all-to-all-start = ((s32[8,1,2]{2,1,0:T(1,128)}), s32[8,1,2]{2,1,0:T(1,128)}, u32[]{:S(2)}, u32[]{:S(2)}) async-start(s32[8,1,2]{2,1,0:T(1,128)} %bitcast.34), calls=%async_computation | async-start | bytes 8192 | tf_op jit(solution)/shard_map/all_to_all | solution.py:147
  19.0 2.1 collective-permute-start.7
  21.2 1.7 gather_fusion.2
  23.9 4.6 %collective-permute-start.6 = (bf16[1,2,1,128,128]{4,3,1,2,0:T(8,128)(2,1)}, bf16[1,2,1,128,128]{4,3,1,2,0:T(8,128)(2,1)}, u32[]{:S(2)}, u32[]{:S(2)}) collective-permute-start(bf16[1,2,1,128,128]{4,3,1,2,0:T(8,128)(2,1)} %get-tuple-element.293), channel_id=1, source_target_pairs={{0,7},{1,6},{2,5},{3,4},{4,3},{5,2},{6,1},{7,0},{8,15},{9,14},{10,... | collective-permute-start | bytes 196616 | tf_op jit(solution)/shard_map/ppermute | solution.py:138
  29.5 1.5 collective-permute-start
  34.0 1.7 sine_convert_fusion.5
  40.5 1.9 convolution_bitcast_fusion.2
  43.0 1.3 gather_fusion.1
  44.3 4.5 %all-to-all-start.1 = ((s32[8,2,2,8]{3,2,1,0:T(2,128)}), s32[8,2,2,8]{3,2,1,0:T(2,128)S(1)}, u32[]{:S(2)}, u32[]{:S(2)}) async-start(s32[8,2,2,8]{3,2,1,0:T(2,128)} %bitcast.35), calls=%async_computation.1 | async-start | bytes 32768 | tf_op jit(solution)/shard_map/all_to_all | solution.py:146
  49.4 1.3 reduce.15
  50.8 2.1 collective-permute-start.1
  52.9 1.5 bitcast_dynamic-update-slice_fusion.6
  54.4 4.9 %collective-permute-done.1 = bf16[1,2,1,128,128]{4,3,1,2,0:T(8,128)(2,1)S(1)} collective-permute-done((bf16[1,2,1,128,128]{4,3,1,2,0:T(8,128)(2,1)}, bf16[1,2,1,128,128]{4,3,1,2,0:T(8,128)(2,1)S(1)}, u32[]{:S(2)}, u32[]{:S(2)}) %collective-permute-start.1) | collective-permute-done | bytes 65568 | tf_op jit(solution)/shard_map/ppermute | solution.py:138
  60.6 7.6 %collective-permute-done.2 = bf16[1,2,1,128,128]{4,3,1,2,0:T(8,128)(2,1)S(1)} collective-permute-done((bf16[1,2,1,128,128]{4,3,1,2,0:T(8,128)(2,1)}, bf16[1,2,1,128,128]{4,3,1,2,0:T(8,128)(2,1)S(1)}, u32[]{:S(2)}, u32[]{:S(2)}) %collective-permute-start.2) | collective-permute-done | bytes 65568 | tf_op jit(solution)/shard_map/ppermute | solution.py:138
  69.5 4.6 %collective-permute-done.3 = bf16[1,2,1,128,128]{4,3,1,2,0:T(8,128)(2,1)S(1)} collective-permute-done((bf16[1,2,1,128,128]{4,3,1,2,0:T(8,128)(2,1)}, bf16[1,2,1,128,128]{4,3,1,2,0:T(8,128)(2,1)S(1)}, u32[]{:S(2)}, u32[]{:S(2)}) %collective-permute-start.3) | collective-permute-done | bytes 65568 | tf_op jit(solution)/shard_map/ppermute | solution.py:138
  74.8 1.5 bitcast_dynamic-update-slice_fusion.2
  76.3 1.5 bitcast_dynamic-update-slice_fusion.1
  77.7 1.5 bitcast_dynamic-update-slice_fusion
  79.2 1.7 gather_fusion.3
  80.9 100.8 %while.24 = (s32[]{:T(128)}, f32[16,1,8]{2,1,0:T(1,128)}, s32[16]{0:T(128)S(1)}, s32[16,2,8]{2,1,0:T(2,128)S(1)}, bf16[16,1,128,128]{3,2,0,1:T(8,128)(2,1)S(1)},...) while((s32[]{:T(128)}, f32[16,1,8]{2,1,0:T(1,128)}, ...), condition=%wide.region_6.7_spmd, body=%wide.region_3.6_spmd.sunk | while | flops 33161740 | bytes 1854074 | solution.py:158
  181.7 4.2 %all-to-all-start.2 = ((f32[8,2,1,8]{3,1,2,0:T(2,128)}), f32[8,2,1,8]{3,1,2,0:T(2,128)S(1)}, u32[]{:S(2)}, u32[]{:S(2)}) async-start(f32[8,2,1,8]{3,1,2,0:T(2,128)} %bitcast.371), calls=%async_computation.2 | async-start | bytes 16384 | tf_op jit(solution)/shard_map/all_to_all | solution.py:166
  186.0 1.3 convolution_bitcast_fusion.4
  189.6 2.9 %all-to-all-done.2 = f32[8,2,1,8]{3,1,2,0:T(2,128)S(1)} async-done(((f32[8,2,1,8]{3,1,2,0:T(2,128)}), f32[8,2,1,8]{3,1,2,0:T(2,128)S(1)}, u32[]{:S(2)}, u32[]{:S(2)}) %all-to-all-start.2) | async-done | bytes 544 | tf_op jit(solution)/shard_map/all_to_all | solution.py:166
  192.4 1.3 gather_fusion.4
  193.7 2.3 gather_fusion.5
  196.2 80.1 %while.25 = (s32[]{:T(128)}, f32[8,8]{1,0:T(8,128)S(1)}, s32[8,2,8]{2,1,0:T(2,128)}, s32[8]{0:T(128)S(1)}, f32[2,256,256]{2,1,0:T(8,128)S(1)}, /*index=5*/bf16[8...) while((s32[]{:T(128)}, f32[8,8]{1,0:T(8,128)S(1)}, ...), condition=%wide.region_10.11_spmd, body=%wide.region_7.10_spmd.sunk | while | flops 232903680 | bytes 6737723 | solution.py:189
  210.5 1.1 sine_convert_fusion.15
  240.6 1.1 sine_convert_fusion.15
  241.7 1.1 sine_convert_fusion.14
  270.6 1.1 sine_convert_fusion.15
  271.7 1.1 sine_convert_fusion.14
  (531 shorter events, 142.0 us)
Async XLA Ops:
  7.2 35.8 %copy-start = (s32[8,2,8]{2,1,0:T(2,128)S(1)}, s32[8,2,8]{2,1,0:T(2,128)}, u32[]{:S(2)}) copy-start(s32[8,2,8]{2,1,0:T(2,128)} %param.16) | copy-start | bytes 1540
  7.2 24.4 %copy-start.13 = (s32[8,1]{0,1:T(1,128)S(1)}, s32[8,1]{0,1:T(1,128)}, u32[]{:S(2)}) copy-start(s32[8,1]{0,1:T(1,128)} %param.14) | copy-start | bytes 100
  7.2 24.4 %copy-start.1 = (s32[8]{0:T(128)S(1)}, s32[8]{0:T(128)}, u32[]{:S(2)}) copy-start(s32[8]{0:T(128)} %param.15) | copy-start | bytes 100
  7.2 186.5 %all-gather.2.cloned.1.call-start = ((), (), s32[]{:S(2)}) async-start(), calls=%async_computation.3 | async-start | bytes 2359296 | tf_op jit(solution)/shard_map/all_gather | solution.py:177
  9.7 22.7 %copy-start.9 = (s32[1024]{0:T(1024)}, s32[1024]{0:T(1024)S(1)}, u32[]{:S(2)}) copy-start(s32[1024]{0:T(1024)S(1)} %pad_clamp_fusion.3) | copy-start | bytes 12292
  11.0 26.4 %copy-start.11 = (s32[2,2,8]{2,1,0:T(2,128)S(1)}, s32[2,2,8]{2,1,0:T(2,128)}, u32[]{:S(2)}) copy-start(s32[2,2,8]{2,1,0:T(2,128)} %param.21) | copy-start | bytes 388
  11.7 32.6 %all-to-all-start = ((s32[8,1,2]{2,1,0:T(1,128)}), s32[8,1,2]{2,1,0:T(1,128)}, u32[]{:S(2)}, u32[]{:S(2)}) async-start(s32[8,1,2]{2,1,0:T(1,128)} %bitcast.34), calls=%async_computation | async-start | bytes 8192 | tf_op jit(solution)/shard_map/all_to_all | solution.py:147
  19.0 166.9 %collective-permute-start.7 = (bf16[2,1,128,128]{3,2,1,0:T(8,128)(2,1)}, bf16[2,1,128,128]{3,2,1,0:T(8,128)(2,1)}, u32[]{:S(2)}, u32[]{:S(2)}) collective-permute-start(bf16[2,1,128,128]{3,2,1,0:T(8,128)(2,1)} %param.20), channel_id=1, source_target_pairs={{0,8},{8,16},{16,24},{1,9},{9,17},{17,25},{2,10},{10,18},{18,26},{... | collective-permute-start | bytes 196616 | tf_op jit(solution)/shard_map/ppermute | solution.py:24
  21.2 18.1 %copy-start.2 = (bf16[8,1,128,128]{3,2,1,0:T(8,128)(2,1)S(1)}, bf16[8,1,128,128]{3,2,1,0:T(8,128)(2,1)}, u32[]{:S(2)}) copy-start(bf16[8,1,128,128]{3,2,1,0:T(8,128)(2,1)} %param.13) | copy-start | bytes 786436
  22.9 17.1 %copy-start.7 = (bf16[2,1,128,128]{3,2,1,0:T(8,128)(2,1)S(1)}, bf16[2,1,128,128]{3,2,1,0:T(8,128)(2,1)}, u32[]{:S(2)}) copy-start(bf16[2,1,128,128]{3,2,1,0:T(8,128)(2,1)} %param.19) | copy-start | bytes 196612
  23.9 53.9 %collective-permute-start.6 = (bf16[1,2,1,128,128]{4,3,1,2,0:T(8,128)(2,1)}, bf16[1,2,1,128,128]{4,3,1,2,0:T(8,128)(2,1)}, u32[]{:S(2)}, u32[]{:S(2)}) collective-permute-start(bf16[1,2,1,128,128]{4,3,1,2,0:T(8,128)(2,1)} %get-tuple-element.293), channel_id=1, source_target_pairs={{0,7},{1,6},{2,5},{3,4},{4,3},{5,2},{6,1},{7,0},{8,15},{9,14},{10,... | collective-permute-start | bytes 196616 | tf_op jit(solution)/shard_map/ppermute | solution.py:138
  28.4 47.9 %collective-permute-start.5 = (bf16[1,2,1,128,128]{4,3,1,2,0:T(8,128)(2,1)}, bf16[1,2,1,128,128]{4,3,1,2,0:T(8,128)(2,1)}, u32[]{:S(2)}, u32[]{:S(2)}) collective-permute-start(bf16[1,2,1,128,128]{4,3,1,2,0:T(8,128)(2,1)} %get-tuple-element.294), channel_id=1, source_target_pairs={{0,6},{1,7},{2,4},{3,5},{4,2},{5,3},{6,0},{7,1},{8,14},{9,15},{10,... | collective-permute-start | bytes 196616 | tf_op jit(solution)/shard_map/ppermute | solution.py:138
  29.0 45.8 %collective-permute-start.4 = (bf16[1,2,1,128,128]{4,3,1,2,0:T(8,128)(2,1)}, bf16[1,2,1,128,128]{4,3,1,2,0:T(8,128)(2,1)}, u32[]{:S(2)}, u32[]{:S(2)}) collective-permute-start(bf16[1,2,1,128,128]{4,3,1,2,0:T(8,128)(2,1)} %get-tuple-element.295), channel_id=1, source_target_pairs={{0,5},{1,4},{2,7},{3,6},{4,1},{5,0},{6,3},{7,2},{8,13},{9,12},{10,... | collective-permute-start | bytes 196616 | tf_op jit(solution)/shard_map/ppermute | solution.py:138
  29.5 21.3 %collective-permute-start = (bf16[1,2,1,128,128]{4,3,1,2,0:T(8,128)(2,1)}, bf16[1,2,1,128,128]{4,3,1,2,0:T(8,128)(2,1)}, u32[]{:S(2)}, u32[]{:S(2)}) collective-permute-start(bf16[1,2,1,128,128]{4,3,1,2,0:T(8,128)(2,1)} %get-tuple-element.299), channel_id=1, source_target_pairs={{0,1},{1,0},{2,3},{3,2},{4,5},{5,4},{6,7},{7,6},{8,9},{9,8},{10,11... | collective-permute-start | bytes 196616 | tf_op jit(solution)/shard_map/ppermute | solution.py:138
  32.7 7.8 %copy-start.3 = (bf16[1,128,128]{2,1,0:T(8,128)(2,1)}, bf16[1,128,128]{2,1,0:T(8,128)(2,1)S(1)}, u32[]{:S(2)}) copy-start(bf16[1,128,128]{2,1,0:T(8,128)(2,1)S(1)} %get-tuple-element.313) | copy-start | bytes 98308
  32.7 7.8 %copy-start.5 = (bf16[1,128,128]{2,1,0:T(8,128)(2,1)}, bf16[1,128,128]{2,1,0:T(8,128)(2,1)S(1)}, u32[]{:S(2)}) copy-start(bf16[1,128,128]{2,1,0:T(8,128)(2,1)S(1)} %get-tuple-element.314) | copy-start | bytes 98308
  42.4 0.6 copy-start.12
  44.3 36.6 %all-to-all-start.1 = ((s32[8,2,2,8]{3,2,1,0:T(2,128)}), s32[8,2,2,8]{3,2,1,0:T(2,128)S(1)}, u32[]{:S(2)}, u32[]{:S(2)}) async-start(s32[8,2,2,8]{3,2,1,0:T(2,128)} %bitcast.35), calls=%async_computation.1 | async-start | bytes 32768 | tf_op jit(solution)/shard_map/all_to_all | solution.py:146
  50.8 8.4 %collective-permute-start.1 = (bf16[1,2,1,128,128]{4,3,1,2,0:T(8,128)(2,1)}, bf16[1,2,1,128,128]{4,3,1,2,0:T(8,128)(2,1)S(1)}, u32[]{:S(2)}, u32[]{:S(2)}) collective-permute-start(bf16[1,2,1,128,128]{4,3,1,2,0:T(8,128)(2,1)} %get-tuple-element.298), channel_id=1, source_target_pairs={{0,2},{1,3},{2,0},{3,1},{4,6},{5,7},{6,4},{7,5},{8,10},{9,11},{10,... | collective-permute-start | bytes 196616 | tf_op jit(solution)/shard_map/ppermute | solution.py:138
  59.2 9.0 %collective-permute-start.2 = (bf16[1,2,1,128,128]{4,3,1,2,0:T(8,128)(2,1)}, bf16[1,2,1,128,128]{4,3,1,2,0:T(8,128)(2,1)S(1)}, u32[]{:S(2)}, u32[]{:S(2)}) collective-permute-start(bf16[1,2,1,128,128]{4,3,1,2,0:T(8,128)(2,1)} %get-tuple-element.297), channel_id=1, source_target_pairs={{0,3},{1,2},{2,1},{3,0},{4,7},{5,6},{6,5},{7,4},{8,11},{9,10},{10,... | collective-permute-start | bytes 196616 | tf_op jit(solution)/shard_map/ppermute | solution.py:138
  68.3 5.9 %collective-permute-start.3 = (bf16[1,2,1,128,128]{4,3,1,2,0:T(8,128)(2,1)}, bf16[1,2,1,128,128]{4,3,1,2,0:T(8,128)(2,1)S(1)}, u32[]{:S(2)}, u32[]{:S(2)}) collective-permute-start(bf16[1,2,1,128,128]{4,3,1,2,0:T(8,128)(2,1)} %get-tuple-element.296), channel_id=1, source_target_pairs={{0,4},{1,5},{2,6},{3,7},{4,0},{5,1},{6,2},{7,3},{8,12},{9,13},{10,... | collective-permute-start | bytes 196616 | tf_op jit(solution)/shard_map/ppermute | solution.py:138
  80.9 105.0 %copy-start.4 = (bf16[1,128,128]{2,1,0:T(8,128)(2,1)S(1)}, bf16[1,128,128]{2,1,0:T(8,128)(2,1)}, u32[]{:S(2)}) copy-start(bf16[1,128,128]{2,1,0:T(8,128)(2,1)} %copy-done.3) | copy-start | bytes 98308
  80.9 105.0 %copy-start.6 = (bf16[1,128,128]{2,1,0:T(8,128)(2,1)S(1)}, bf16[1,128,128]{2,1,0:T(8,128)(2,1)}, u32[]{:S(2)}) copy-start(bf16[1,128,128]{2,1,0:T(8,128)(2,1)} %copy-done.5) | copy-start | bytes 98308
  181.7 6.6 %copy-start.8 = (s32[2,1,1,8]{3,2,0,1:T(1,128)S(1)}, s32[2,1,1,8]{3,2,0,1:T(1,128)}, u32[]{:S(2)}) copy-start(s32[2,1,1,8]{3,2,0,1:T(1,128)} %get-tuple-element.307) | copy-start | bytes 196
  181.7 10.7 %all-to-all-start.2 = ((f32[8,2,1,8]{3,1,2,0:T(2,128)}), f32[8,2,1,8]{3,1,2,0:T(2,128)S(1)}, u32[]{:S(2)}, u32[]{:S(2)}) async-start(f32[8,2,1,8]{3,1,2,0:T(2,128)} %bitcast.371), calls=%async_computation.2 | async-start | bytes 16384 | tf_op jit(solution)/shard_map/all_to_all | solution.py:166
  187.3 8.8 %copy-start.10 = (pred[8]{0:T(512)(128)(4,1)S(1)}, pred[8]{0:T(512)(128)(4,1)}, u32[]{:S(2)}) copy-start(pred[8]{0:T(512)(128)(4,1)} %get-tuple-element.265) | copy-start | bytes 28
  193.7 2.5 copy-start.14
  193.7 2.5 copy-start.16
  276.3 0.6 copy-start.15
Sparse Core Ops, SparseCore 0:
  10.2 59.1 all-gather.1
